TPU v7x, 256 devices: a whole 4x4x8 slice. The times are simulated.
256 devices in a mesh: ctx: 64 (over x, y, z_hi, core), chan: 4 (over z_lo).
Axes of the slice: x: 4, y: 4, z: 8 (z_hi: 2, z_lo: 4; z = z_hi * 4 + z_lo), core: 2. Of those that a mesh axis runs over, the one named last changes fastest.
Arguments:
- query_proj: bfloat16 [24576, 4096], P('ctx', 'chan'), may hold values from -6 to 6
- key_proj: bfloat16 [24576, 4096], P('ctx', 'chan'), may hold values from -6 to 6
- value_proj: bfloat16 [24576, 4096], P('ctx', 'chan'), may hold values from -6 to 6
- filter_taps: float32 [24576, 4096], P('ctx', 'chan'), may hold values from -1.1 to 1.1
- skip_gain: float32 [4096], P('chan'), may hold values from -4 to 4
- out_weight: bfloat16 [4096, 4096], P('chan'), may hold values from -0.09375 to 0.09375
Outputs:
- mixed_out: bfloat16 [24576, 4096], P('ctx', 'chan')
All inputs are finite; a program needn't handle non-finite values.
Results may differ from a plain program's by a relative error of at most 0.0049.
Values may be sent and summed in bfloat16 or wider, within the bound.
A program may use at most 128 MiB of HBM per device.

v0:
```python
import math

import jax
import jax.numpy as jnp
from jax import lax
from jax.sharding import PartitionSpec as P

HIGHEST_PREC = lax.Precision.HIGHEST


def angles(first_idx, second_idx, modulus):
    turned = first_idx * second_idx % modulus
    phase = turned.astype(jnp.float32) * (2.0 * math.pi / modulus)
    return (jnp.cos(phase), jnp.sin(phase))


def index_grid(count_a, count_b, axis_pick):
    return lax.broadcasted_iota(jnp.int32, (count_a, count_b), axis_pick)


def spectral_product(spectra, inverse_scale):
    sig_re = spectra[0, 0]
    sig_im = spectra[1, 0]
    filt_re = spectra[0, 1]
    filt_im = spectra[1, 1]
    prod_re = (sig_re * filt_re - sig_im * filt_im) * inverse_scale
    prod_im = (sig_re * filt_im + sig_im * filt_re) * inverse_scale
    return jnp.stack([prod_re, prod_im], 0)


def local_conv(columns, outer_len, inner_len):
    half_len = outer_len // 2
    width = columns.shape[2]
    full_len = outer_len * inner_len
    grid = columns.reshape(2, half_len, inner_len, width)
    cos_outer, sin_outer = angles(
        index_grid(outer_len, half_len, 0), index_grid(outer_len, half_len, 1), outer_len
    )
    first_re = jnp.einsum("kn,snac->skac", cos_outer, grid, precision=HIGHEST_PREC)
    first_im = -jnp.einsum("kn,snac->skac", sin_outer, grid, precision=HIGHEST_PREC)
    cos_twist, sin_twist = angles(
        index_grid(outer_len, inner_len, 0), index_grid(outer_len, inner_len, 1), full_len
    )
    cos_wide = cos_twist[:, :, None]
    sin_wide = sin_twist[:, :, None]
    turned_re = first_re * cos_wide + first_im * sin_wide
    turned_im = first_im * cos_wide - first_re * sin_wide
    cos_inner, sin_inner = angles(
        index_grid(inner_len, inner_len, 0), index_grid(inner_len, inner_len, 1), inner_len
    )
    spec_re = jnp.einsum(
        "ma,skac->skmc", cos_inner, turned_re, precision=HIGHEST_PREC
    ) + jnp.einsum("ma,skac->skmc", sin_inner, turned_im, precision=HIGHEST_PREC)
    spec_im = jnp.einsum(
        "ma,skac->skmc", cos_inner, turned_im, precision=HIGHEST_PREC
    ) - jnp.einsum("ma,skac->skmc", sin_inner, turned_re, precision=HIGHEST_PREC)
    product = spectral_product(jnp.stack([spec_re, spec_im], 0), 1.0 / full_len)
    back_re = jnp.einsum("am,kmc->kac", cos_inner, product[0], precision=HIGHEST_PREC) - jnp.einsum(
        "am,kmc->kac", sin_inner, product[1], precision=HIGHEST_PREC
    )
    back_im = jnp.einsum("am,kmc->kac", cos_inner, product[1], precision=HIGHEST_PREC) + jnp.einsum(
        "am,kmc->kac", sin_inner, product[0], precision=HIGHEST_PREC
    )
    untwist_re = back_re * cos_wide - back_im * sin_wide
    untwist_im = back_im * cos_wide + back_re * sin_wide
    result = jnp.einsum("kn,kac->nac", cos_outer, untwist_re, precision=HIGHEST_PREC) - jnp.einsum(
        "kn,kac->nac", sin_outer, untwist_im, precision=HIGHEST_PREC
    )
    return result.reshape(half_len * inner_len, width)


def per_device(query_proj, key_proj, value_proj, filter_taps, skip_gain, out_weight):
    group_size = lax.axis_size("ctx")
    tok_rows = query_proj.shape[0]
    block_count = 2 * group_size
    signal = key_proj.astype(jnp.float32) * value_proj.astype(jnp.float32)
    both = jnp.stack([signal, filter_taps], 0)
    columns = lax.all_to_all(both, "ctx", split_axis=2, concat_axis=1, tiled=True)
    conv_columns = local_conv(columns, tok_rows, block_count)
    conv = lax.all_to_all(conv_columns, "ctx", split_axis=0, concat_axis=1, tiled=True)
    gated = (query_proj.astype(jnp.float32) * (conv + skip_gain[None, :] * signal)).astype(
        jnp.bfloat16
    )
    partial_sums = jnp.dot(gated, out_weight, preferred_element_type=jnp.float32)
    return lax.psum_scatter(partial_sums, "chan", scatter_dimension=1, tiled=True).astype(
        jnp.bfloat16
    )


def solution(mesh):
    placed = (
        P("ctx", "chan"),
        P("ctx", "chan"),
        P("ctx", "chan"),
        P("ctx", "chan"),
        P("chan"),
        P("chan", None),
    )
    return jax.shard_map(
        per_device, mesh=mesh, in_specs=placed, out_specs=P("ctx", "chan"), check_vma=False
    )
```

profile of v0, /device:TPU:1, one launch (start us, length us, event | category | flops | bytes accessed | tf_op | source)
XLA Modules:
  0.0 382.1 jit_solution(15431643375483112326)
XLA Ops:
  6.5 1.5 copy.28
  8.0 1.8 copy.29
  9.8 2.2 copy.30
  12.4 4.1 %copy.31 = f32[2,384,1024]{1,0,2:T(2,128)} copy(f32[2,384,1024]{1,2,0:T(8,128)S(1)} %pad_maximum_fusion) | data formatting | bytes 6291456 | tf_op jit(solution)/shard_map/stack | solution.py:77
  16.4 15.6 %all-to-all-start = ((f32[2,384,1024]{1,0,2:T(2,128)}), f32[2,384,1024]{1,0,2:T(2,128)S(1)}, u32[]{:S(2)}, u32[]{:S(2)}) async-start(f32[2,384,1024]{1,0,2:T(2,128)} %copy.31), calls=%async_computation | async-start | bytes 6291456 | tf_op jit(solution)/shard_map/all_to_all | solution.py:78
  32.1 0.8 fusion.63
  32.9 0.8 copy.38
  33.7 0.8 copy.39
  34.5 75.3 %all-to-all-done = f32[2,384,1024]{1,0,2:T(2,128)S(1)} async-done(((f32[2,384,1024]{1,0,2:T(2,128)}), f32[2,384,1024]{1,0,2:T(2,128)S(1)}, u32[]{:S(2)}, u32[]{:S(2)}) %all-to-all-start) | async-done | bytes 3145760 | tf_op jit(solution)/shard_map/all_to_all | solution.py:78
  110.0 2.6 copy.33
  112.6 2.8 reshape.62
  115.4 7.9 %fusion.44 = f32[2,128,16,384]{3,1,2,0:T(8,128)S(1)} fusion(f32[2,192,128,16]{2,1,3,0:T(8,128)S(1)} %reshape.62), kind=kOutput, calls=%fused_computation.47 | convolution fusion | flops 3624542208 | bytes 9437184 | tf_op jit(solution)/shard_map/kn,snac->skac/dot_general | solution.py:40
  123.3 8.1 %fusion.46 = f32[2,128,16,384]{3,1,2,0:T(8,128)S(1)} fusion(f32[2,192,128,16]{2,1,3,0:T(8,128)S(1)} %reshape.62), kind=kOutput, calls=%fused_computation.49 | convolution fusion | flops 3624542208 | bytes 9437184 | tf_op jit(solution)/shard_map/kn,snac->skac/dot_general | solution.py:39
  131.4 11.0 %fusion.40 = f32[2,384,16,128]{3,1,2,0:T(8,128)S(1)} fusion(f32[2,128,16,384]{3,1,2,0:T(8,128)S(1)} %fusion.46, f32[2,128,16,384]{3,1,2,0:T(8,128)S(1)} %fusion.44, f32[384,128]{0,1:T(8,128)S(1)} %get-tuple-element.7, f32[384,128]{0,1:T(8,128)S(1)} %get-tuple-element.8), kind=kOutput, calls=%fused_computation.42 | convolution fusion | flops 2422439936 | bytes 19267584 | tf_op jit(solution)/shard_map/ma,skac->skmc/dot_general | solution.py:51
  142.4 12.6 %fusion.36 = f32[2,384,16,128]{3,1,2,0:T(8,128)} fusion(f32[2,128,16,384]{3,1,2,0:T(8,128)S(1)} %fusion.46, f32[2,128,16,384]{3,1,2,0:T(8,128)S(1)} %fusion.44, f32[384,128]{0,1:T(8,128)S(1)} %get-tuple-element.7, f32[384,128]{0,1:T(8,128)S(1)} %get-tuple-element.8), kind=kOutput, calls=%fused_computation.41 | convolution fusion | flops 2422439936 | bytes 19267584 | tf_op jit(solution)/shard_map/ma,skac->skmc/dot_general | solution.py:54
  155.0 10.6 %add_bitcast_fusion = f32[1,2,384,128,16]{3,2,4,1,0:T(8,128)S(1)} fusion(f32[2,384,16,128]{3,1,2,0:T(8,128)S(1)} %fusion.40, f32[2,128,16,384]{3,1,2,0:T(8,128)S(1)} %fusion.46, f32[2,128,16,384]{3,1,2,0:T(8,128)S(1)} %fusion.44, f32[384,128]{0,1:T(8,128)S(1)} %get-tuple-element.7, f32[384,128]{0,1:T(8,128)S(1)} %get-tuple-element.8), kind=kOutput, calls=%fused_computation.7 | convolution fusion | flops 2424012800 | bytes 25559040 | tf_op jit(solution)/shard_map/ma,skac->skmc/dot_general | solution.py:53
  165.6 13.5 %subtract_bitcast_fusion = f32[1,2,384,128,16]{3,2,4,1,0:T(8,128)S(1)} fusion(f32[2,384,16,128]{3,1,2,0:T(8,128)} %fusion.36, f32[2,128,16,384]{3,1,2,0:T(8,128)S(1)} %fusion.46, f32[2,128,16,384]{3,1,2,0:T(8,128)S(1)} %fusion.44, f32[384,128]{0,1:T(8,128)S(1)} %get-tuple-element.7, f32[384,128]{0,1:T(8,128)S(1)} %get-tuple-element.8), kind=kOutput, calls=%fused_computation.6 | convolution fusion | flops 2424012800 | bytes 25559040 | tf_op jit(solution)/shard_map/ma,skac->skmc/dot_general | solution.py:56
  179.1 1.6 subtract_multiply_fusion
  180.7 3.0 fusion.6
  183.7 3.0 fusion.8
  186.6 3.0 fusion.23
  189.6 3.2 fusion.20
  192.9 4.1 %fusion.2 = f32[192,128,16]{1,0,2:T(8,128)S(1)} fusion(f32[384,16,128]{2,0,1:T(8,128)S(1)} %fusion.20, f32[384,16,128]{2,0,1:T(8,128)S(1)} %fusion.23, f32[384,128]{1,0:T(8,128)S(1)} %copy-done.5, f32[384,128]{1,0:T(8,128)S(1)} %copy-done.4), kind=kOutput, calls=%fused_computation.9 | convolution fusion | flops 1814962176 | bytes 8257536 | tf_op jit(solution)/shard_map/kn,kac->nac/dot_general | solution.py:66
  197.0 4.2 %fusion.32 = f32[192,128,16]{1,0,2:T(8,128)S(1)} fusion(f32[192,128,16]{1,0,2:T(8,128)S(1)} %fusion.2, f32[384,16,128]{2,0,1:T(8,128)S(1)} %fusion.23, f32[384,16,128]{2,0,1:T(8,128)S(1)} %fusion.20, f32[384,128]{1,0:T(8,128)S(1)} %copy-done.5, f32[384,128]{1,0:T(8,128)S(1)} %copy-done.4), kind=kOutput, calls=%fused_computation.39 | convolution fusion | flops 1815355392 | bytes 9830400 | tf_op jit(solution)/shard_map/kn,kac->nac/dot_general | solution.py:66
  201.6 2.1 copy.40
  203.7 4.4 %all-to-all-start.1 = ((f32[64,384,16]{1,2,0:T(8,128)}), f32[64,384,16]{1,2,0:T(8,128)S(1)}, u32[]{:S(2)}, u32[]{:S(2)}) async-start(f32[64,384,16]{1,2,0:T(8,128)} %copy.40), calls=%async_computation.1 | async-start | bytes 3145728 | tf_op jit(solution)/shard_map/all_to_all | solution.py:80
  208.3 2.3 copy.27
  210.6 24.2 %all-to-all-done.1 = f32[64,384,16]{1,2,0:T(8,128)S(1)} async-done(((f32[64,384,16]{1,2,0:T(8,128)}), f32[64,384,16]{1,2,0:T(8,128)S(1)}, u32[]{:S(2)}, u32[]{:S(2)}) %all-to-all-start.1) | async-done | bytes 1572896 | tf_op jit(solution)/shard_map/all_to_all | solution.py:80
  234.8 1.7 fusion.27
  236.6 9.5 %fusion.146 = f32[384,4096]{1,0:T(8,128)} fusion(bf16[384,1024]{0,1:T(8,128)(2,1)S(1)} %fusion.27, bf16[1024,4096]{1,0:T(8,128)(2,1)} %param.11), kind=kOutput, calls=%fused_computation.138 | convolution fusion | flops 3221225472 | bytes 15466496 | tf_op jit(solution)/shard_map/dot_general | solution.py:84
  246.1 126.5 %reduce-scatter.2.cloned.1.call-done = f32[384,1024]{1,0:T(8,128)} async-done(((f32[384,4096]{1,0:T(8,128)}), f32[384,1024]{1,0:T(8,128)}) %reduce-scatter.2.cloned.1.call-update) | async-done | bytes 1572880 | tf_op jit(solution)/shard_map/reduce_scatter | solution.py:85
  372.6 2.4 convert_element_type.79
  (20 shorter events, 1.2 us)
Async XLA Ops:
  8.0 4.1 %copy-start = (bf16[384,1024]{0,1:T(8,128)(2,1)}, bf16[384,1024]{0,1:T(8,128)(2,1)S(1)}, u32[]{:S(2)}) copy-start(bf16[384,1024]{0,1:T(8,128)(2,1)S(1)} %copy.28) | copy-start | bytes 2359300
  9.8 2.4 copy-start.2
  16.4 93.3 %all-to-all-start = ((f32[2,384,1024]{1,0,2:T(2,128)}), f32[2,384,1024]{1,0,2:T(2,128)S(1)}, u32[]{:S(2)}, u32[]{:S(2)}) async-start(f32[2,384,1024]{1,0,2:T(2,128)} %copy.31), calls=%async_computation | async-start | bytes 6291456 | tf_op jit(solution)/shard_map/all_to_all | solution.py:78
  189.6 3.3 copy-start.4
  189.6 3.3 copy-start.5
  203.7 31.2 %copy-start.1 = (bf16[384,1024]{0,1:T(8,128)(2,1)S(1)}, bf16[384,1024]{0,1:T(8,128)(2,1)}, u32[]{:S(2)}) copy-start(bf16[384,1024]{0,1:T(8,128)(2,1)} %copy-done) | copy-start | bytes 2359300
  203.7 31.2 %copy-start.3 = (bf16[384,1024]{0,1:T(8,128)(2,1)S(1)}, bf16[384,1024]{0,1:T(8,128)(2,1)}, u32[]{:S(2)}) copy-start(bf16[384,1024]{0,1:T(8,128)(2,1)} %copy-done.2) | copy-start | bytes 2359300
  203.7 31.2 %copy-start.6 = (f32[1024]{0:T(1024)S(1)}, f32[1024]{0:T(1024)}, u32[]{:S(2)}) copy-start(f32[1024]{0:T(1024)} %param.10) | copy-start | bytes 12292
  203.7 31.2 %all-to-all-start.1 = ((f32[64,384,16]{1,2,0:T(8,128)}), f32[64,384,16]{1,2,0:T(8,128)S(1)}, u32[]{:S(2)}, u32[]{:S(2)}) async-start(f32[64,384,16]{1,2,0:T(8,128)} %copy.40), calls=%async_computation.1 | async-start | bytes 3145728 | tf_op jit(solution)/shard_map/all_to_all | solution.py:80
  208.0 164.6 %reduce-scatter.2.cloned.1.call-start = ((), (), s32[]{:S(2)}) async-start(), calls=%async_computation.3 | async-start | bytes 7864320 | tf_op jit(solution)/shard_map/reduce_scatter | solution.py:85
Sparse Core Ops, SparseCore 0:
  246.2 126.3 reduce-scatter.1
where the time goes:
time: 388 us; the launch traced here: 382 us
  waiting for transfers between devices  226 us (58%)
  matrix products  93.6 us (24%)
  local copies, waits for them, and re-layouts  21.5 us (6%)
  starting transfers between devices  20.2 us (5%)
  between operations  13.9 us (4%)
  other arithmetic  6.87 us (2%)
    reduce_scatter x1, waiting for transfers between devices, per_device(): lax.psum_scatter(partial_sums, 'chan', scatter_dimension=1, tiled=True)  127 us
    all_to_all x1, waiting for transfers between devices, per_device(): lax.all_to_all(both, 'ctx', split_axis=2, concat_axis=1, tiled=True)  75.3 us
    all_to_all x1, waiting for transfers between devices, per_device(): lax.all_to_all(conv_columns, 'ctx', split_axis=0, concat_axis=1, tiled=True)  24.2 us
    all_to_all x1, starting transfers between devices, per_device(): lax.all_to_all(both, 'ctx', split_axis=2, concat_axis=1, tiled=True)  15.6 us
    dot_general x1, matrix products, local_conv(): jnp.einsum('ma,skac->skmc', sin_inner, turned_re, precision=HIGHEST_PREC)  13.5 us
    dot_general x1, matrix products, local_conv(): jnp.einsum('ma,skac->skmc', cos_inner, turned_im, precision=HIGHEST_PREC)  12.6 us
    dot_general x1, matrix products, local_conv(): jnp.einsum('ma,skac->skmc', cos_inner, turned_re, precision=HIGHEST_PREC)  11 us
    dot_general x1, matrix products, local_conv(): jnp.einsum('ma,skac->skmc', sin_inner, turned_im, precision=HIGHEST_PREC)  10.6 us
  transfers between devices with their start and end apart: 3, of which 3 were waited for; matrix products, arithmetic and copies ran while one was open for 1% of the time, Pallas kernels for 0%

commit v1 on v0

v1 whole, which is shorter than its diff:
```python
import functools
import math

import jax
import jax.numpy as jnp
import numpy as np
import ml_dtypes
from jax import lax
from jax.experimental import pallas as pl
from jax.experimental.pallas import tpu as pltpu
from jax.sharding import PartitionSpec as P

BF16 = jnp.bfloat16
F32 = jnp.float32
LANE = 128


def split_const(table):
    high = table.astype(np.float32).astype(ml_dtypes.bfloat16)
    low = (table - high.astype(np.float64)).astype(np.float32).astype(ml_dtypes.bfloat16)
    return high, low


def dft_tables(blocks, tok_rows):
    sub = tok_rows // LANE
    half = blocks * sub
    outer = 2 * half
    full = outer * LANE
    order = (np.arange(blocks)[None, :] * sub + np.arange(sub)[:, None]).reshape(-1)
    freq = np.arange(half) + 0.5
    phase = 2.0 * math.pi * ((order[None, :] * (2 * np.arange(half)[:, None] + 1)) % (2 * outer)) / (2 * outer)
    first = np.concatenate([np.cos(phase), -np.sin(phase)], 0)
    back = np.concatenate([np.cos(phase).T, -np.sin(phase).T], 1) * (2.0 / full)
    turn = 2.0 * math.pi * np.arange(LANE)[None, :] * freq[:, None] / full
    inner = 2.0 * math.pi * ((np.arange(LANE)[:, None] * np.arange(LANE)[None, :]) % LANE) / LANE
    c, s = np.cos(inner), np.sin(inner)
    forward = np.block([[c, -s], [s, c]])
    inverse = np.block([[c, s], [-s, c]])
    return (
        *split_const(first),
        *split_const(forward),
        *split_const(inverse),
        *split_const(back),
        np.cos(turn).astype(np.float32),
        np.sin(turn).astype(np.float32),
    )


def dot(a, b):
    return jnp.dot(a, b, preferred_element_type=F32)


def split(x):
    high = x.astype(BF16)
    low = (x - high.astype(F32)).astype(BF16)
    return high, low


def dot3(x, m_hi, m_lo):
    hi, lo = split(x)
    return dot(hi, m_hi) + dot(lo, m_hi) + dot(hi, m_lo)


def prep_kernel(k_ref, v_ref, f_ref, s_out, f_out):
    s = k_ref[...].astype(F32) * v_ref[...].astype(F32)
    s_out[...] = s.T.astype(BF16)
    f_out[...] = f_ref[...].T.astype(BF16)


def prep(k, v, f):
    rows, width = k.shape
    step = 256
    spec = pl.BlockSpec((rows, step), lambda i: (0, i))
    out = pl.BlockSpec((step, rows), lambda i: (i, 0))
    shape = jax.ShapeDtypeStruct((width, rows), BF16)
    return pl.pallas_call(
        prep_kernel,
        grid=(width // step,),
        in_specs=[spec] * 3,
        out_specs=[out, out],
        out_shape=[shape, shape],
    )(k, v, f)


def conv_kernel(
    blocks, group, sub,
    s_ref, f_ref, a_hi, a_lo, fw_hi, fw_lo, iv_hi, iv_lo, bk_hi, bk_lo, cos_ref, sin_ref,
    out_ref, s_wide, f_wide, o_wide,
):
    half = blocks * sub
    for a in range(sub):
        s_wide[a] = s_ref[:, a * LANE:(a + 1) * LANE].astype(F32)
        f_wide[a] = f_ref[:, a * LANE:(a + 1) * LANE].astype(F32)

    def columns(wide, c):
        parts = [
            wide.at[a][pl.ds(c, blocks, stride=group), :] for a in range(sub)
        ]
        return jnp.concatenate(parts, 0).astype(BF16)

    def step(p, _):
        chans = (2 * p, 2 * p + 1)
        x = jnp.concatenate(
            [columns(s_wide, c) for c in chans] + [columns(f_wide, c) for c in chans], 1
        )
        y = dot(a_hi[...], x) + dot(a_lo[...], x)
        cos, sin = cos_ref[...], sin_ref[...]
        spectra = []
        for j in range(4):
            re = y[:half, j * LANE:(j + 1) * LANE]
            im = y[half:, j * LANE:(j + 1) * LANE]
            turned = jnp.concatenate([re * cos + im * sin, im * cos - re * sin], 1)
            spectra.append(dot3(turned, fw_hi[...], fw_lo[...]))
        backs = []
        for j in range(2):
            s, f = spectra[j], spectra[2 + j]
            s_re, s_im, f_re, f_im = s[:, :LANE], s[:, LANE:], f[:, :LANE], f[:, LANE:]
            product = jnp.concatenate([s_re * f_re - s_im * f_im, s_re * f_im + s_im * f_re], 1)
            g = dot3(product, iv_hi[...], iv_lo[...])
            re, im = g[:, :LANE], g[:, LANE:]
            backs.append(jnp.concatenate([re * cos - im * sin, im * cos + re * sin], 0))
        z_hi, z_lo = split(jnp.concatenate(backs, 1))
        res = dot(bk_hi[...], z_hi) + dot(bk_hi[...], z_lo) + dot(bk_lo[...], z_hi)
        for j, c in enumerate(chans):
            for a in range(sub):
                o_wide.at[a][pl.ds(c, blocks, stride=group), :] = res[
                    a * blocks:(a + 1) * blocks, j * LANE:(j + 1) * LANE
                ]
        return 0

    lax.fori_loop(0, group // 2, step, 0)
    for a in range(sub):
        out_ref[:, a * LANE:(a + 1) * LANE] = o_wide[a].astype(BF16)


def long_conv(s, f, blocks):
    total, rows = s.shape
    group = total // blocks
    sub = rows // LANE
    tables = dft_tables(blocks, rows)
    wide = pltpu.VMEM((sub, total, LANE), F32)
    return pl.pallas_call(
        functools.partial(conv_kernel, blocks, group, sub),
        out_shape=jax.ShapeDtypeStruct((total, rows), BF16),
        scratch_shapes=[wide, wide, wide],
        compiler_params=pltpu.CompilerParams(vmem_limit_bytes=48 * 1024 * 1024),
    )(s, f, *[jnp.asarray(t) for t in tables])


def gate_kernel(c_ref, q_ref, k_ref, v_ref, g_ref, out_ref):
    signal = k_ref[...].astype(F32) * v_ref[...].astype(F32)
    conv = c_ref[...].astype(F32).T
    out_ref[...] = (q_ref[...].astype(F32) * (conv + g_ref[...] * signal)).astype(BF16)


def gate(conv, q, k, v, gain):
    rows, width = q.shape
    step = 256
    spec = pl.BlockSpec((rows, step), lambda i: (0, i))
    return pl.pallas_call(
        gate_kernel,
        grid=(width // step,),
        in_specs=[
            pl.BlockSpec((step, rows), lambda i: (i, 0)),
            spec, spec, spec,
            pl.BlockSpec((1, step), lambda i: (0, i)),
        ],
        out_specs=spec,
        out_shape=jax.ShapeDtypeStruct((rows, width), BF16),
    )(conv, q, k, v, gain)


def per_device(query_proj, key_proj, value_proj, filter_taps, skip_gain, out_weight):
    blocks = lax.axis_size("ctx")
    s, f = prep(key_proj, value_proj, filter_taps)
    s = lax.all_to_all(s, "ctx", split_axis=0, concat_axis=0, tiled=True)
    f = lax.all_to_all(f, "ctx", split_axis=0, concat_axis=0, tiled=True)
    conv = long_conv(s, f, blocks)
    conv = lax.all_to_all(conv, "ctx", split_axis=0, concat_axis=0, tiled=True)
    gated = gate(conv, query_proj, key_proj, value_proj, skip_gain[None, :])
    partial_sums = jnp.dot(gated, out_weight, preferred_element_type=F32).astype(BF16)
    return lax.psum_scatter(partial_sums, "chan", scatter_dimension=1, tiled=True)


def solution(mesh):
    placed = (
        P("ctx", "chan"),
        P("ctx", "chan"),
        P("ctx", "chan"),
        P("ctx", "chan"),
        P("chan"),
        P("chan", None),
    )
    return jax.shard_map(
        per_device, mesh=mesh, in_specs=placed, out_specs=P("ctx", "chan"), check_vma=False
    )
```

time: 388 us -> 210 us (0.54); the launches traced: 382 us -> 209 us
  waiting for transfers between devices: 226 us -> 67.6 us
  blocking collectives: 0 us -> 89.1 us
  matrix products: 93.6 us -> 8.68 us
  Pallas kernels: 0 us -> 21.2 us
  starting transfers between devices: 20.2 us -> 0.01 us
  local copies, waits for them, and re-layouts: 21.5 us -> 9.07 us
  other arithmetic: 6.87 us -> 0 us
    all_to_all x2 -> x0, waiting for transfers between devices: 99.5 us -> none  [the longest x1 75.3 us: per_device(): lax.all_to_all(both, 'ctx', split_axis=2, concat_axis=1, tiled=True)]
    all_to_all x0 -> x3, blocking collectives: none -> 89.1 us  [the longest x1 42.5 us: per_device(): f = lax.all_to_all(f, 'ctx', split_axis=0, concat_axis=0, tiled=True)]
    dot_general x13 -> x1, matrix products: 93.6 us -> 8.68 us  [per_device(): jnp.dot(gated, out_weight, preferred_element_type=F32).astype(BF16)]
    reduce_scatter x1, waiting for transfers between devices: 127 us -> 67.5 us  [per_device(): lax.psum_scatter(partial_sums, 'chan', scatter_dimension=1, tiled=True)]
    pallas_call x0 -> x3, Pallas kernels: none -> 21.2 us  [the longest x1 13 us: long_conv(): pl.pallas_call(functools.partial(conv_kernel, blocks, group, sub), out_sh...]
    all_to_all x2 -> x0, starting transfers between devices: 20 us -> none  [the longest x1 15.6 us: per_device(): lax.all_to_all(both, 'ctx', split_axis=2, concat_axis=1, tiled=True)]
    all_to_all x4 -> x0, local copies, waits for them, and re-layouts: 5.21 us -> none  [the longest x2 2.77 us: per_device(): lax.all_to_all(both, 'ctx', split_axis=2, concat_axis=1, tiled=True)]
    convert_element_type x2 -> x0, other arithmetic: 4.13 us -> none  [the longest x1 2.41 us: per_device(): lax.psum_scatter(partial_sums, 'chan', scatter_dimension=1, tiled=True)]
  transfers between devices with their start and end apart: 3 -> 1, of which waited for: 3 -> 1; matrix products, arithmetic and copies ran while one was open for 1% -> 0% of each run, Pallas kernels for 0% -> 0%
where the time goes in v1:
time: 210 us; the launch traced here: 209 us
  blocking collectives  89.1 us (42%)
  waiting for transfers between devices  67.6 us (32%)
  Pallas kernels  21.2 us (10%)
  between operations  13.4 us (6%)
  local copies, waits for them, and re-layouts  9.07 us (4%)
  matrix products  8.68 us (4%)
    reduce_scatter x1, waiting for transfers between devices, per_device(): lax.psum_scatter(partial_sums, 'chan', scatter_dimension=1, tiled=True)  67.5 us
    all_to_all x1, blocking collectives, per_device(): f = lax.all_to_all(f, 'ctx', split_axis=0, concat_axis=0, tiled=True)  42.5 us
    all_to_all x1, blocking collectives, per_device(): conv = lax.all_to_all(conv, 'ctx', split_axis=0, concat_axis=0, tiled=True)  24 us
    all_to_all x1, blocking collectives, per_device(): s = lax.all_to_all(s, 'ctx', split_axis=0, concat_axis=0, tiled=True)  22.6 us
    pallas_call x1, Pallas kernels, long_conv(): pl.pallas_call(functools.partial(conv_kernel, blocks, group, sub), out_sh...  13 us
    unnamed x20, local copies, waits for them, and re-layouts  9.07 us
    dot_general x1, matrix products, per_device(): jnp.dot(gated, out_weight, preferred_element_type=F32).astype(BF16)  8.68 us
  transfers between devices with their start and end apart: 1, of which 1 were waited for; matrix products, arithmetic and copies ran while one was open for 0% of the time, Pallas kernels for 0%

profile of v1, /device:TPU:1, one launch (start us, length us, event | category | flops | bytes accessed | tf_op | source)
XLA Modules:
  0.0 209.0 jit_solution(427572946668192543)
XLA Ops:
  6.5 0.0 reduce-scatter.2.cloned.1.call-start
  6.5 4.2 %shard_map.154 = (bf16[1024,384]{1,0:T(8,128)(2,1)}, bf16[1024,384]{1,0:T(8,128)(2,1)}) custom-call(bf16[384,1024]{1,0:T(8,128)(2,1)} %k_ref.3, bf16[384,1024]{1,0:T(8,128)(2,1)} %v_ref.3, f32[384,1024]{1,0:T(8,128)} %f_ref.1), custom_call_target="tpu_custom_call" | custom-call | tf_op jit(solution)/shard_map/pallas_call | solution.py:76
  10.7 42.5 %all_to_all.33 = bf16[64,16,384]{2,1,0:T(8,128)(2,1)S(1)} all-to-all(bf16[64,16,384]{2,1,0:T(8,128)(2,1)} %bitcast.14), channel_id=1, replica_groups=mesh['ctx'=64,'chan'=4] {'ctx'}, dimensions={0} | all-to-all | bytes 1572864 | tf_op jit(solution)/shard_map/all_to_all | solution.py:177
  53.1 22.6 %all_to_all.34 = bf16[64,16,384]{2,1,0:T(8,128)(2,1)S(1)} all-to-all(bf16[64,16,384]{2,1,0:T(8,128)(2,1)} %bitcast.13), channel_id=1, replica_groups=mesh['ctx'=64,'chan'=4] {'ctx'}, dimensions={0} | all-to-all | bytes 1572864 | tf_op jit(solution)/shard_map/all_to_all | solution.py:176
  75.8 0.0 copy-start
  75.8 0.9 copy-done
  76.7 0.0 copy-start.1
  76.7 0.9 copy-done.1
  77.6 0.0 copy-start.2
  77.6 0.9 copy-done.2
  78.5 0.0 copy-start.3
  78.5 0.9 copy-done.3
  79.4 0.0 copy-start.4
  79.4 0.9 copy-done.4
  80.3 0.0 copy-start.5
  80.3 0.9 copy-done.5
  81.2 0.0 copy-start.6
  81.2 0.9 copy-done.6
  82.2 0.0 copy-start.7
  82.2 0.9 copy-done.7
  83.1 0.0 copy-start.8
  83.1 0.9 copy-done.8
  83.9 0.0 copy-start.9
  84.0 0.9 copy-done.9
  84.8 13.0 %shard_map.155 = bf16[1024,384]{1,0:T(8,128)(2,1)S(1)} custom-call(bf16[1024,384]{1,0:T(8,128)(2,1)S(1)} %bitcast.10, bf16[1024,384]{1,0:T(8,128)(2,1)S(1)} %bitcast.9, bf16[384,192]{1,0:T(8,128)(2,1)S(1)} %copy-done.1, bf16[384,192]{1,0:T(8,128)(2,1)S(1)} %copy-done, bf16[256,256]{1,0:T(8,128)(2,1)S(1)} %copy-done.7, bf16[256,256]{1,0:T(8,128)(2,1)S(1)} %copy-done.6, ...), custom_call_target="tpu_custom_call" | custom-call | tf_op jit(solution)/shard_map/pallas_call | solution.py:142
  97.9 24.0 %all_to_all.35 = bf16[64,16,384]{2,1,0:T(8,128)(2,1)} all-to-all(bf16[64,16,384]{2,1,0:T(8,128)(2,1)S(1)} %bitcast.11), channel_id=1, replica_groups=mesh['ctx'=64,'chan'=4] {'ctx'}, dimensions={0} | all-to-all | bytes 1572864 | tf_op jit(solution)/shard_map/all_to_all | solution.py:179
  121.9 4.0 %shard_map.156 = bf16[384,1024]{1,0:T(8,128)(2,1)} custom-call(bf16[1024,384]{1,0:T(8,128)(2,1)} %bitcast.12, bf16[384,1024]{1,0:T(8,128)(2,1)} %q_ref.1, bf16[384,1024]{1,0:T(8,128)(2,1)} %k_ref.3, bf16[384,1024]{1,0:T(8,128)(2,1)} %v_ref.3, f32[1,1024]{1,0:T(1,128)} %bitcast.15), custom_call_target="tpu_custom_call" | custom-call | tf_op jit(solution)/shard_map/pallas_call | solution.py:160
  125.9 8.7 %convolution_convert_fusion = bf16[384,4096]{1,0:T(8,128)(2,1)} fusion(bf16[384,1024]{1,0:T(8,128)(2,1)} %shard_map.156, bf16[1024,4096]{1,0:T(8,128)(2,1)} %param.21), kind=kOutput, calls=%fused_computation | convolution fusion | flops 3222798336 | bytes 12320768 | tf_op jit(solution)/shard_map/dot_general | solution.py:181
  134.6 0.0 reduce-scatter.2.cloned.1.call-update
  134.6 67.5 %reduce-scatter.2.cloned.1.call-done = bf16[384,1024]{1,0:T(8,128)(2,1)} async-done(((bf16[384,4096]{1,0:T(8,128)(2,1)}), bf16[384,1024]{1,0:T(8,128)(2,1)}) %reduce-scatter.2.cloned.1.call-update) | async-done | bytes 786448 | tf_op jit(solution)/shard_map/reduce_scatter | solution.py:182
Async XLA Ops:
  6.5 195.7 %reduce-scatter.2.cloned.1.call-start = ((), (), s32[]{:S(2)}) async-start(), calls=%async_computation.4 | async-start | bytes 3932160 | tf_op jit(solution)/shard_map/reduce_scatter | solution.py:182
  75.8 0.9 copy-start
  76.7 0.9 copy-start.1
  77.6 0.9 copy-start.2
  78.5 0.9 copy-start.3
  79.4 0.9 copy-start.4
  80.3 0.9 copy-start.5
  81.2 0.9 copy-start.6
  82.2 0.9 copy-start.7
  83.1 0.9 copy-start.8
  83.9 0.9 copy-start.9
Sparse Core Ops, SparseCore 0:
  134.8 67.3 reduce-scatter.1

commit v2 on v1

v2 whole, which is shorter than its diff:
```python
import functools
import math

import jax
import jax.numpy as jnp
import numpy as np
import ml_dtypes
from jax import lax
from jax.experimental import pallas as pl
from jax.experimental.pallas import tpu as pltpu
from jax.sharding import PartitionSpec as P

BF16 = jnp.bfloat16
F32 = jnp.float32
LANE = 128


def split_const(table):
    high = table.astype(np.float32).astype(ml_dtypes.bfloat16)
    low = (table - high.astype(np.float64)).astype(np.float32).astype(ml_dtypes.bfloat16)
    return high, low


def dft_tables(blocks, tok_rows):
    sub = tok_rows // LANE
    half = blocks * sub
    outer = 2 * half
    full = outer * LANE
    order = (np.arange(blocks)[None, :] * sub + np.arange(sub)[:, None]).reshape(-1)
    freq = np.arange(half) + 0.5
    phase = 2.0 * math.pi * ((order[None, :] * (2 * np.arange(half)[:, None] + 1)) % (2 * outer)) / (2 * outer)
    first = np.concatenate([np.cos(phase), -np.sin(phase)], 0)
    back = np.concatenate([np.cos(phase).T, -np.sin(phase).T], 1) * (2.0 / full)
    turn = 2.0 * math.pi * np.arange(LANE)[None, :] * freq[:, None] / full
    inner = 2.0 * math.pi * ((np.arange(LANE)[:, None] * np.arange(LANE)[None, :]) % LANE) / LANE
    c, s = np.cos(inner), np.sin(inner)
    forward = np.block([[c, -s], [s, c]])
    inverse = np.block([[c, s], [-s, c]])
    return (
        *split_const(first),
        *split_const(forward),
        *split_const(inverse),
        *split_const(back),
        np.cos(turn).astype(np.float32),
        np.sin(turn).astype(np.float32),
    )


def dot(a, b):
    return jnp.dot(a, b, preferred_element_type=F32)


def split(x):
    high = x.astype(BF16)
    low = (x - high.astype(F32)).astype(BF16)
    return high, low


def dot3(x, m_hi, m_lo):
    hi, lo = split(x)
    return dot(hi, m_hi) + dot(lo, m_hi) + dot(hi, m_lo)


MESH = pl.DeviceIdType.MESH
COLS = 256


def whole_kernel(
    blocks, group, sub, width,
    q_hbm, k_hbm, v_hbm, f_hbm, gain_hbm, w_hbm,
    first_hi, first_lo, fw_hi_in, fw_lo_in, iv_hi_in, iv_lo_in, bk_hi_in, bk_lo_in, cos_in, sin_in,
    out_hbm,
    q_v, k_v, v_v, f_v, gain_v, w_own, w_near,
    a_hi, a_lo, fw_hi, fw_lo, iv_hi, iv_lo, bk_hi, bk_lo, cos_ref, sin_ref,
    send_f, send_s, send_c, recv_f, recv_s, recv_c,
    wide_a, wide_b, spec_f,
    g_own, g_near, part_out, part_in, part_own, out_v,
    load_sem, table_sem, own_sem, store_sem,
    a2a_send, a2a_recv, wz_send, wz_recv, wx_send, wx_recv, wc_send, wc_recv,
    g_send, g_recv, p_send, p_recv,
):
    c = lax.axis_index("ctx")
    h = lax.axis_index("chan")
    near = h + 1 - 2 * lax.rem(h, 2)
    far = lax.rem(h + 2, 4)
    far_near = lax.rem(near + 2, 4)
    core = lax.rem(c, 2)
    sibling = c + 1 - 2 * core
    plane = lax.rem(c, 4)
    spot = lax.div(c, 4)
    spots = blocks // 4
    rows = sub * LANE
    half = blocks * sub
    slab = width // blocks * 2

    bar = pltpu.get_barrier_semaphore()

    def greet(j, _):
        pl.semaphore_signal(
            bar, inc=1, device_id=(lax.rem(c + j, blocks), h), device_id_type=MESH
        )
        return 0

    loads = [
        pltpu.make_async_copy(src, dst, load_sem.at[i])
        for i, (src, dst) in enumerate(
            [
                (f_hbm, f_v),
                (k_hbm, k_v),
                (v_hbm, v_v),
                (q_hbm, q_v),
                (gain_hbm, gain_v),
                (w_hbm.at[:, pl.ds(pl.multiple_of(h * width, width), width)], w_own.at[:, pl.ds(0, width)]),
                (w_hbm.at[:, pl.ds(pl.multiple_of(far * width, width), width)], w_own.at[:, pl.ds(width, width)]),
            ]
        )
    ]
    tables = [
        pltpu.make_async_copy(src, dst, table_sem.at[i])
        for i, (src, dst) in enumerate(
            zip(
                (first_hi, first_lo, fw_hi_in, fw_lo_in, iv_hi_in, iv_lo_in, bk_hi_in, bk_lo_in, cos_in, sin_in),
                (a_hi, a_lo, fw_hi, fw_lo, iv_hi, iv_lo, bk_hi, bk_lo, cos_ref, sin_ref),
            )
        )
    ]
    for copy in loads[:3]:
        copy.start()
    lax.fori_loop(1, blocks, greet, 0)
    for other in (near, far):
        pl.semaphore_signal(bar, inc=1, device_id=(c, other), device_id_type=MESH)
    for copy in loads[3:] + tables:
        copy.start()

    def a2a_copy(i, src, dst, j):
        to = lax.rem(c + j, blocks)
        return pltpu.make_async_remote_copy(
            src_ref=src.at[pl.ds(pl.multiple_of(to * group, group), group)],
            dst_ref=dst.at[pl.ds(pl.multiple_of(c * group, group), group)],
            send_sem=a2a_send.at[i],
            recv_sem=a2a_recv.at[i],
            device_id=(to, h),
            device_id_type=MESH,
        )

    def own_copy(i, src, dst):
        mine = pl.ds(pl.multiple_of(c * group, group), group)
        return pltpu.make_async_copy(src.at[mine], dst.at[mine], own_sem.at[i])

    def a2a_start(i, src, dst):
        def send(j, _):
            a2a_copy(i, src, dst, j).start()
            return 0

        own_copy(i, src, dst).start()
        lax.fori_loop(1, blocks, send, 0)

    def a2a_all(i, src, dst):
        most = pl.ds(0, (blocks - 1) * group)
        return pltpu.make_async_remote_copy(
            src_ref=src.at[most],
            dst_ref=dst.at[most],
            send_sem=a2a_send.at[i],
            recv_sem=a2a_recv.at[i],
            device_id=(sibling, h),
            device_id_type=MESH,
        )

    def a2a_arrived(i, src, dst):
        own_copy(i, src, dst).wait()
        a2a_all(i, src, dst).wait_recv()

    loads[0].wait()
    for i in range(width // COLS):
        send_f[i * COLS:(i + 1) * COLS, :] = f_v[:, i * COLS:(i + 1) * COLS].T.astype(BF16)
    pl.semaphore_wait(bar, blocks + 1)

    my_rows = pl.ds(pl.multiple_of(core * (width // 2) + spot * slab, slab), slab)

    def near_slice(i, block):
        return pltpu.make_async_remote_copy(
            src_ref=w_hbm.at[my_rows, pl.ds(pl.multiple_of(block * width, width), width)],
            dst_ref=w_near.at[my_rows, pl.ds(i * width, width)],
            send_sem=wz_send.at[i],
            recv_sem=wz_recv.at[i],
            device_id=(c, near),
            device_id_type=MESH,
        )

    near_copies = [near_slice(0, near), near_slice(1, far_near)]
    for copy in near_copies:
        copy.start()
    a2a_start(0, send_f, recv_f)

    loads[1].wait()
    loads[2].wait()
    for i in range(width // COLS):
        piece = slice(i * COLS, (i + 1) * COLS)
        signal = k_v[:, piece].astype(F32) * v_v[:, piece].astype(F32)
        send_s[piece, :] = signal.T.astype(BF16)
    a2a_start(1, send_s, recv_s)

    for copy in near_copies:
        copy.wait_recv()

    def spread(j, _):
        to = lax.rem(spot + j, spots) * 4 + plane
        pltpu.make_async_remote_copy(
            src_ref=w_near.at[my_rows],
            dst_ref=w_near.at[my_rows],
            send_sem=wx_send,
            recv_sem=wx_recv,
            device_id=(to, h),
            device_id_type=MESH,
        ).start()
        return 0

    lax.fori_loop(1, spots, spread, 0)
    spread_rows = pl.ds(0, (spots - 1) * slab)
    spread_all = pltpu.make_async_remote_copy(
        src_ref=w_near.at[spread_rows],
        dst_ref=w_near.at[spread_rows],
        send_sem=wx_send,
        recv_sem=wx_recv,
        device_id=(sibling, h),
        device_id_type=MESH,
    )
    core_rows = pl.ds(pl.multiple_of(core * (width // 2), width // 2), width // 2)
    to_sibling = pltpu.make_async_remote_copy(
        src_ref=w_near.at[core_rows],
        dst_ref=w_near.at[core_rows],
        send_sem=wc_send,
        recv_sem=wc_recv,
        device_id=(sibling, h),
        device_id_type=MESH,
    )

    for copy in tables:
        copy.wait()

    def widen(src, wide):
        for a in range(sub):
            wide[a] = src[:, a * LANE:(a + 1) * LANE].astype(F32)

    def columns(wide, ch):
        parts = [wide.at[a][pl.ds(ch, blocks, stride=group), :] for a in range(sub)]
        return jnp.concatenate(parts, 0).astype(BF16)

    def spectra(wide, chans):
        x = jnp.concatenate([columns(wide, ch) for ch in chans], 1)
        y = dot(a_hi[...], x) + dot(a_lo[...], x)
        cos, sin = cos_ref[...], sin_ref[...]
        found = []
        for j in range(len(chans)):
            re = y[:half, j * LANE:(j + 1) * LANE]
            im = y[half:, j * LANE:(j + 1) * LANE]
            turned = jnp.concatenate([re * cos + im * sin, im * cos - re * sin], 1)
            found.append(dot3(turned, fw_hi[...], fw_lo[...]))
        return found

    a2a_arrived(0, send_f, recv_f)
    widen(recv_f, wide_a)

    def taps_step(p, _):
        chans = (2 * p, 2 * p + 1)
        for ch, spec in zip(chans, spectra(wide_a, chans)):
            spec_f[ch] = spec
        return 0

    lax.fori_loop(0, group // 2, taps_step, 0)

    a2a_arrived(1, send_s, recv_s)
    widen(recv_s, wide_a)

    def conv_step(p, _):
        chans = (2 * p, 2 * p + 1)
        cos, sin = cos_ref[...], sin_ref[...]
        backs = []
        for ch, s in zip(chans, spectra(wide_a, chans)):
            f = spec_f[ch]
            s_re, s_im, f_re, f_im = s[:, :LANE], s[:, LANE:], f[:, :LANE], f[:, LANE:]
            product = jnp.concatenate([s_re * f_re - s_im * f_im, s_re * f_im + s_im * f_re], 1)
            g = dot3(product, iv_hi[...], iv_lo[...])
            re, im = g[:, :LANE], g[:, LANE:]
            backs.append(jnp.concatenate([re * cos - im * sin, im * cos + re * sin], 0))
        z_hi, z_lo = split(jnp.concatenate(backs, 1))
        res = dot(bk_hi[...], z_hi) + dot(bk_hi[...], z_lo) + dot(bk_lo[...], z_hi)
        for j, ch in enumerate(chans):
            for a in range(sub):
                wide_b.at[a][pl.ds(ch, blocks, stride=group), :] = res[
                    a * blocks:(a + 1) * blocks, j * LANE:(j + 1) * LANE
                ]
        return 0

    lax.fori_loop(0, group // 2, conv_step, 0)
    for a in range(sub):
        send_c[:, a * LANE:(a + 1) * LANE] = wide_b[a].astype(BF16)
    a2a_start(2, send_c, recv_c)

    spread_all.wait_recv()
    to_sibling.start()
    for copy in loads[3:]:
        copy.wait()
    a2a_arrived(2, send_c, recv_c)

    swaps = []
    for t in range(sub):
        here = slice(t * LANE, (t + 1) * LANE)
        for i in range(width // COLS):
            piece = slice(i * COLS, (i + 1) * COLS)
            conv = recv_c[piece, here].astype(F32).T
            signal = k_v[here, piece].astype(F32) * v_v[here, piece].astype(F32)
            g_own[t, :, piece] = (
                q_v[here, piece].astype(F32) * (conv + gain_v[:, piece] * signal)
            ).astype(BF16)
        swap = pltpu.make_async_remote_copy(
            src_ref=g_own.at[t],
            dst_ref=g_near.at[t],
            send_sem=g_send.at[t],
            recv_sem=g_recv.at[t],
            device_id=(c, near),
            device_id_type=MESH,
        )
        swap.start()
        swaps.append(swap)

    to_sibling.wait_recv()
    parts = []
    for t in range(sub):
        swaps[t].wait_recv()

        def project(i, _, t=t):
            cols = pl.ds(pl.multiple_of(width + i * COLS, COLS), COLS)
            part_out[t, :, pl.ds(pl.multiple_of(i * COLS, COLS), COLS)] = (
                dot(g_own[t], w_own[:, cols]) + dot(g_near[t], w_near[:, cols])
            ).astype(BF16)
            return 0

        lax.fori_loop(0, width // COLS, project, 0)
        part = pltpu.make_async_remote_copy(
            src_ref=part_out.at[t],
            dst_ref=part_in.at[t],
            send_sem=p_send.at[t],
            recv_sem=p_recv.at[t],
            device_id=(c, far),
            device_id_type=MESH,
        )
        part.start()
        parts.append(part)
    for t in range(sub):

        def project_own(i, _, t=t):
            cols = pl.ds(pl.multiple_of(i * COLS, COLS), COLS)
            part_own[t, :, cols] = dot(g_own[t], w_own[:, cols]) + dot(g_near[t], w_near[:, cols])
            return 0

        lax.fori_loop(0, width // COLS, project_own, 0)
    stores = []
    for t in range(sub):
        parts[t].wait_recv()
        out_v[t] = (part_own[t] + part_in[t].astype(F32)).astype(BF16)
        store = pltpu.make_async_copy(
            out_v.at[t], out_hbm.at[pl.ds(t * LANE, LANE)], store_sem.at[t]
        )
        store.start()
        stores.append(store)

    for store in stores:
        store.wait()
    for i, (src, dst) in enumerate([(send_f, recv_f), (send_s, recv_s), (send_c, recv_c)]):
        a2a_all(i, src, dst).wait_send()
    for copy in near_copies + [spread_all, to_sibling] + swaps + parts:
        copy.wait_send()


def per_device(query_proj, key_proj, value_proj, filter_taps, skip_gain, out_weight):
    blocks = lax.axis_size("ctx")
    rows, width = query_proj.shape
    group = width // blocks
    sub = rows // LANE
    half = blocks * sub
    tables = [jnp.asarray(t) for t in dft_tables(blocks, rows)]
    gain = skip_gain[None, :]
    dma = pltpu.SemaphoreType.DMA

    def like(x):
        return pltpu.VMEM(x.shape, x.dtype)

    flat = pltpu.VMEM((width, rows), BF16)
    wide = pltpu.VMEM((sub, width, LANE), F32)
    weights = pltpu.VMEM((width, 2 * width), BF16)
    piece = pltpu.VMEM((sub, LANE, width), BF16)
    return pl.pallas_call(
        functools.partial(whole_kernel, blocks, group, sub, width),
        out_shape=jax.ShapeDtypeStruct((rows, width), BF16),
        in_specs=[pl.BlockSpec(memory_space=pl.ANY)] * (6 + len(tables)),
        out_specs=pl.BlockSpec(memory_space=pl.ANY),
        scratch_shapes=[
            like(query_proj), like(key_proj), like(value_proj), like(filter_taps), like(gain),
            weights, weights,
            *[like(t) for t in tables],
            *[flat] * 6,
            wide, wide, pltpu.VMEM((group, half, 2 * LANE), F32),
            piece, piece, piece, piece, pltpu.VMEM((sub, LANE, width), F32), piece,
            dma((7,)), dma((len(tables),)), dma((3,)), dma((sub,)),
            dma((3,)), dma((3,)), dma((2,)), dma((2,)), dma, dma, dma, dma,
            dma((sub,)), dma((sub,)), dma((sub,)), dma((sub,)),
        ],
        compiler_params=pltpu.CompilerParams(
            collective_id=0, has_side_effects=True, vmem_limit_bytes=56 * 1024 * 1024
        ),
    )(query_proj, key_proj, value_proj, filter_taps, gain, out_weight, *tables)


def solution(mesh):
    placed = (
        P("ctx", "chan"),
        P("ctx", "chan"),
        P("ctx", "chan"),
        P("ctx", "chan"),
        P("chan"),
        P("chan", None),
    )
    return jax.shard_map(
        per_device, mesh=mesh, in_specs=placed, out_specs=P("ctx", "chan"), check_vma=False
    )
```

time: 210 us -> 135 us (0.64)
  the two profiles are of different devices: /device:TPU:1 before, /device:TPU:102 now
where the time goes in v2:
time: 135 us
  Pallas kernels  133 us (99%)
  local copies, waits for them, and re-layouts  2.06 us (2%)
    pallas_call x1, Pallas kernels, per_device(): pl.pallas_call(functools.partial(whole_kernel, blocks, group, sub, width)...  133 us

profile of v2, /device:TPU:102, one launch (start us, length us, event | category | flops | bytes accessed | tf_op | source)
XLA Modules:
  0.0 135.0 jit_solution(10779163558331963914)
XLA Ops:
  0.0 132.9 %shard_map.154 = bf16[384,1024]{1,0:T(8,128)(2,1)} custom-call(bf16[384,1024]{1,0:T(8,128)(2,1)} %q_hbm.1, bf16[384,1024]{1,0:T(8,128)(2,1)} %k_hbm.1, bf16[384,1024]{1,0:T(8,128)(2,1)} %v_hbm.1, f32[384,1024]{1,0:T(8,128)} %f_hbm.1, f32[1,1024]{1,0:T(1,128)} %bitcast.1, bf16[1024,4096]{1,0:T(8,128)(2,1)} %w_hbm.1, ...), custom_call_target="tpu_custom_call" | custom-call | tf_op jit(solution)/shard_map/pallas_call | solution.py:393
  132.9 2.1 %copy.18 = bf16[384,1024]{1,0:T(8,128)(2,1)} copy(bf16[384,1024]{1,0:T(8,128)(2,1)} %shard_map.154) | data formatting | bytes 1572864

commit v3 on v2

v3 whole, which is shorter than its diff:
```python
import functools
import math

import jax
import jax.numpy as jnp
import numpy as np
import ml_dtypes
from jax import lax
from jax.experimental import pallas as pl
from jax.experimental.pallas import tpu as pltpu
from jax.sharding import PartitionSpec as P

BF16 = jnp.bfloat16
F32 = jnp.float32
LANE = 128


def split_const(table):
    high = table.astype(np.float32).astype(ml_dtypes.bfloat16)
    low = (table - high.astype(np.float64)).astype(np.float32).astype(ml_dtypes.bfloat16)
    return high, low


def dft_tables(chips, runs):
    sub = 2 * runs
    half = chips * sub
    outer = 2 * half
    full = outer * LANE
    run, core, chip = np.meshgrid(np.arange(runs), np.arange(2), np.arange(chips), indexing="ij")
    order = (chip * sub + core * runs + run).reshape(-1)
    freq = np.arange(half) + 0.5
    phase = 2.0 * math.pi * ((order[None, :] * (2 * np.arange(half)[:, None] + 1)) % (2 * outer)) / (2 * outer)
    first = np.concatenate([np.cos(phase), -np.sin(phase)], 0)
    back = np.concatenate([np.cos(phase).T, -np.sin(phase).T], 1) * (2.0 / full)
    turn = 2.0 * math.pi * np.arange(LANE)[None, :] * freq[:, None] / full
    inner = 2.0 * math.pi * ((np.arange(LANE)[:, None] * np.arange(LANE)[None, :]) % LANE) / LANE
    c, s = np.cos(inner), np.sin(inner)
    forward = np.block([[c, -s], [s, c]])
    inverse = np.block([[c, s], [-s, c]])
    return (
        *split_const(first),
        *split_const(forward),
        *split_const(inverse),
        *split_const(back),
        np.cos(turn).astype(np.float32),
        np.sin(turn).astype(np.float32),
    )


def dot(a, b):
    return jnp.dot(a, b, preferred_element_type=F32)


def split(x):
    high = x.astype(BF16)
    low = (x - high.astype(F32)).astype(BF16)
    return high, low


def dot3(x, m_hi, m_lo):
    hi, lo = split(x)
    return dot(hi, m_hi) + dot(lo, m_hi) + dot(hi, m_lo)


MESH = pl.DeviceIdType.MESH
COLS = 256
SETS = 2
PART = 8


def whole_kernel(
    chips, runs, width,
    q_hbm, k_hbm, v_hbm, f_hbm, gain_hbm, w_hbm,
    first_hi, first_lo, fw_hi_in, fw_lo_in, iv_hi_in, iv_lo_in, bk_hi_in, bk_lo_in, cos_in, sin_in,
    out_hbm,
    q_v, k_v, v_v, f_v, gain_v, w_own, w_near,
    a_hi, a_lo, fw_hi, fw_lo, iv_hi, iv_lo, bk_hi, bk_lo, cos_ref, sin_ref,
    keep_f, keep_s, give_f, give_s, give_c, take_f, take_s, take_c,
    send_f, send_s, send_c, recv_f, recv_s, recv_c,
    wide_a, wide_b, spec_f,
    g_own, g_near, part_out, part_in, part_own, out_v,
    load_sem, table_sem, own_sem, store_sem,
    a2a_send, a2a_recv, x_send, x_recv, wz_send, wz_recv, wx_send, wx_recv, wc_send, wc_recv,
    g_send, g_recv, p_send, p_recv,
):
    c = lax.axis_index("ctx")
    h = lax.axis_index("chan")
    near = h + 1 - 2 * lax.rem(h, 2)
    far = lax.rem(h + 2, 4)
    far_near = lax.rem(near + 2, 4)
    core = lax.rem(c, 2)
    chip = lax.div(c, 2)
    sibling = c + 1 - 2 * core
    plane = lax.rem(c, 4)
    spot = lax.div(c, 4)
    spots = chips // 2
    half = chips * runs * 2
    side = width // 2
    tall = runs * 2 * PART
    slab = side // spots

    bar = pltpu.get_barrier_semaphore()

    def peer(j):
        return lax.rem(chip + j, chips) * 2 + core

    def greet(j, _):
        pl.semaphore_signal(bar, inc=1, device_id=(peer(j), h), device_id_type=MESH)
        return 0

    def block_cols(block):
        return pl.ds(pl.multiple_of(block * width, width), width)

    loads = [
        pltpu.make_async_copy(src, dst, load_sem.at[i])
        for i, (src, dst) in enumerate(
            [
                (f_hbm, f_v),
                (k_hbm, k_v),
                (v_hbm, v_v),
                (q_hbm, q_v),
                (gain_hbm, gain_v),
                (w_hbm.at[:, block_cols(h)], w_own.at[0]),
                (w_hbm.at[:, block_cols(far)], w_own.at[1]),
            ]
        )
    ]
    tables = [
        pltpu.make_async_copy(src, dst, table_sem.at[i])
        for i, (src, dst) in enumerate(
            zip(
                (first_hi, first_lo, fw_hi_in, fw_lo_in, iv_hi_in, iv_lo_in, bk_hi_in, bk_lo_in, cos_in, sin_in),
                (a_hi, a_lo, fw_hi, fw_lo, iv_hi, iv_lo, bk_hi, bk_lo, cos_ref, sin_ref),
            )
        )
    ]
    for copy in loads[:3]:
        copy.start()
    lax.fori_loop(1, chips, greet, 0)
    pl.semaphore_signal(bar, inc=1, device_id=(sibling, h), device_id_type=MESH)
    for other in (near, far):
        pl.semaphore_signal(bar, inc=1, device_id=(c, other), device_id_type=MESH)
    for copy in loads[3:] + tables:
        copy.start()

    def remote(src, dst, send, recv, device):
        return pltpu.make_async_remote_copy(
            src_ref=src, dst_ref=dst, send_sem=send, recv_sem=recv,
            device_id=device, device_id_type=MESH,
        )

    moves = [(send_f, recv_f, slice(0, SETS), (0, tall))]
    moves += [(send_s, recv_s, slice(g, g + 1), (0, tall)) for g in range(SETS)]
    moves += [(send_c, recv_c, slice(0, 1), (0, tall))]
    moves += [(send_c, recv_c, slice(1, 2), (a * 2 * PART, 2 * PART)) for a in range(runs)]

    def view(ref, i, first, count):
        _, _, sets, (start, size) = moves[i]
        return ref.at[sets, pl.ds(first, count), pl.ds(start, size), :]

    def a2a_own(i):
        src, dst = moves[i][:2]
        return pltpu.make_async_copy(view(src, i, chip, 1), view(dst, i, chip, 1), own_sem.at[i])

    def a2a_start(i):
        src, dst = moves[i][:2]

        def send(j, _):
            to = peer(j)
            remote(
                view(src, i, lax.rem(chip + j, chips), 1), view(dst, i, chip, 1),
                a2a_send.at[i], a2a_recv.at[i], (to, h),
            ).start()
            return 0

        a2a_own(i).start()
        lax.fori_loop(1, chips, send, 0)

    def a2a_all(i):
        src, dst = moves[i][:2]
        return remote(
            view(src, i, 0, chips - 1), view(dst, i, 0, chips - 1),
            a2a_send.at[i], a2a_recv.at[i], (sibling, h),
        )

    def a2a_arrived(i):
        a2a_own(i).wait()
        a2a_all(i).wait_recv()

    def swap_cores(i, src, dst):
        return remote(src, dst, x_send.at[i], x_recv.at[i], (sibling, h))

    mine = pl.multiple_of(core * side, side)
    theirs = pl.multiple_of(side - core * side, side)

    def turn(fetch, keep, give):
        for a in range(runs):
            here = slice(a * LANE, (a + 1) * LANE)
            for start, dst in ((theirs, give), (mine, keep)):
                for i in range(side // COLS):
                    cols = pl.ds(pl.multiple_of(start + i * COLS, COLS), COLS)
                    dst[a, i * COLS:(i + 1) * COLS, :] = fetch(here, cols).T.astype(BF16)

    def assemble(keep, take, dst):
        for a in range(runs):
            own = keep[a].astype(F32).reshape(chips, SETS, PART, LANE)
            got = take[a].astype(F32).reshape(chips, SETS, PART, LANE)
            for g in range(SETS):
                both = jnp.concatenate([own[:, g], got[:, g]], 1)
                dst[g, :, a * 2 * PART:(a + 1) * 2 * PART, :] = both.astype(BF16)

    loads[0].wait()
    turn(lambda here, cols: f_v[here, cols], keep_f, give_f)
    pl.semaphore_wait(bar, chips + 2)
    swap_f = swap_cores(0, give_f, take_f)
    swap_f.start()

    my_rows = pl.ds(pl.multiple_of(core * side + spot * slab, slab), slab)

    def near_slice(i, block):
        return remote(
            w_hbm.at[my_rows, block_cols(block)], w_near.at[i, my_rows],
            wz_send.at[i], wz_recv.at[i], (c, near),
        )

    near_copies = [near_slice(0, near), near_slice(1, far_near)]
    for copy in near_copies:
        copy.start()
    loads[1].wait()
    loads[2].wait()
    turn(
        lambda here, cols: k_v[here, cols].astype(F32) * v_v[here, cols].astype(F32), keep_s, give_s
    )
    swap_s = swap_cores(1, give_s, take_s)
    swap_s.start()
    swap_f.wait_recv()
    assemble(keep_f, take_f, send_f)
    a2a_start(0)
    swap_s.wait_recv()
    assemble(keep_s, take_s, send_s)
    for g in range(SETS):
        a2a_start(1 + g)

    def spread(i):
        def send(j, _):
            to = lax.rem(spot + j, spots) * 4 + plane
            remote(
                w_near.at[i, my_rows], w_near.at[i, my_rows], wx_send.at[i], wx_recv.at[i], (to, h)
            ).start()
            return 0

        near_copies[i].wait_recv()
        lax.fori_loop(1, spots, send, 0)

    def spread_all(i):
        most = pl.ds(0, (spots - 1) * slab)
        return remote(
            w_near.at[i, most], w_near.at[i, most], wx_send.at[i], wx_recv.at[i], (sibling, h)
        )

    def to_sibling(i):
        rows = pl.ds(mine, side)
        return remote(
            w_near.at[i, rows], w_near.at[i, rows], wc_send.at[i], wc_recv.at[i], (sibling, h)
        )

    spread(1)

    for copy in tables:
        copy.wait()

    def places(a, ch, at):
        return pl.ds(a * 2 * PART + lax.rem(core + at, 2) * PART + ch, chips, stride=tall)

    def columns(wide, ch):
        parts = [wide[places(a, ch, at), :] for a in range(runs) for at in range(2)]
        return jnp.concatenate(parts, 0).astype(BF16)

    def spectra(wide, chans):
        x = jnp.concatenate([columns(wide, ch) for ch in chans], 1)
        y = dot(a_hi[...], x) + dot(a_lo[...], x)
        cos, sin = cos_ref[...], sin_ref[...]
        found = []
        for j in range(len(chans)):
            re = y[:half, j * LANE:(j + 1) * LANE]
            im = y[half:, j * LANE:(j + 1) * LANE]
            turned = jnp.concatenate([re * cos + im * sin, im * cos - re * sin], 1)
            found.append(dot3(turned, fw_hi[...], fw_lo[...]))
        return found

    def widen(src):
        wide_a[...] = src.astype(F32).reshape(chips * tall, LANE)

    a2a_arrived(0)
    for g in range(SETS):
        widen(recv_f[g])

        def taps_step(p, _, g=g):
            chans = (2 * p, 2 * p + 1)
            for ch, spec in zip(chans, spectra(wide_a, chans)):
                spec_f[g * PART + ch] = spec
            return 0

        lax.fori_loop(0, PART // 2, taps_step, 0)

    for g in range(SETS):
        a2a_arrived(1 + g)
        widen(recv_s[g])

        def conv_step(p, _, g=g):
            chans = (2 * p, 2 * p + 1)
            cos, sin = cos_ref[...], sin_ref[...]
            backs = []
            for ch, s in zip(chans, spectra(wide_a, chans)):
                f = spec_f[g * PART + ch]
                s_re, s_im, f_re, f_im = s[:, :LANE], s[:, LANE:], f[:, :LANE], f[:, LANE:]
                product = jnp.concatenate([s_re * f_re - s_im * f_im, s_re * f_im + s_im * f_re], 1)
                z = dot3(product, iv_hi[...], iv_lo[...])
                re, im = z[:, :LANE], z[:, LANE:]
                backs.append(jnp.concatenate([re * cos - im * sin, im * cos + re * sin], 0))
            z_hi, z_lo = split(jnp.concatenate(backs, 1))
            res = dot(bk_hi[...], z_hi) + dot(bk_hi[...], z_lo) + dot(bk_lo[...], z_hi)
            for j, ch in enumerate(chans):
                for a in range(runs):
                    for at in range(2):
                        row = (2 * a + at) * chips
                        wide_b[places(a, ch, at), :] = res[
                            row:row + chips, j * LANE:(j + 1) * LANE
                        ]
            return 0

        lax.fori_loop(0, PART // 2, conv_step, 0)
        send_c[g] = wide_b[...].reshape(chips, tall, LANE).astype(BF16)
        for i in (range(3, 4) if g == 0 else range(4, 4 + runs)):
            a2a_start(i)

    spread_all(1).wait_recv()
    to_sibling(1).start()
    for copy in loads[3:]:
        copy.wait()

    def gated(a, conv, start):
        here = slice(a * LANE, (a + 1) * LANE)
        for i in range(side // COLS):
            cols = pl.ds(pl.multiple_of(start + i * COLS, COLS), COLS)
            signal = k_v[here, cols].astype(F32) * v_v[here, cols].astype(F32)
            turned = conv[i * COLS:(i + 1) * COLS, :].T
            g_own[a, :, cols] = (
                q_v[here, cols].astype(F32) * (turned + gain_v[:, cols] * signal)
            ).astype(BF16)

    a2a_arrived(3)
    swaps = []
    backs = []
    for a in range(runs):
        a2a_arrived(4 + a)
        tile = [recv_c[g, :, a * 2 * PART:(a + 1) * 2 * PART, :].astype(F32) for g in range(SETS)]
        other = jnp.concatenate([t[:, PART:] for t in tile], 1).reshape(side, LANE)
        give_c[a] = other.astype(BF16)
        back = swap_cores(2 + a, give_c.at[a], take_c.at[a])
        back.start()
        backs.append(back)
        own = jnp.concatenate([t[:, :PART] for t in tile], 1).reshape(side, LANE)
        gated(a, own, mine)
        back.wait_recv()
        gated(a, take_c[a].astype(F32), theirs)
        swap = remote(g_own.at[a], g_near.at[a], g_send.at[a], g_recv.at[a], (c, near))
        swap.start()
        swaps.append(swap)

    spread(0)

    def product(i, a, piece):
        cols = pl.ds(pl.multiple_of(piece * COLS, COLS), COLS)
        return cols, dot(g_own[a], w_own[i, :, cols]) + dot(g_near[a], w_near[i, :, cols])

    to_sibling(1).wait_recv()
    parts = []
    for a in range(runs):
        swaps[a].wait_recv()

        def project(piece, _, a=a):
            cols, sums = product(1, a, piece)
            part_out[a, :, cols] = sums.astype(BF16)
            return 0

        lax.fori_loop(0, width // COLS, project, 0)
        part = remote(part_out.at[a], part_in.at[a], p_send.at[a], p_recv.at[a], (c, far))
        part.start()
        parts.append(part)
    spread_all(0).wait_recv()
    to_sibling(0).start()
    to_sibling(0).wait_recv()
    for a in range(runs):

        def project_own(piece, _, a=a):
            cols, sums = product(0, a, piece)
            part_own[a, :, cols] = sums
            return 0

        lax.fori_loop(0, width // COLS, project_own, 0)
    stores = []
    for a in range(runs):
        parts[a].wait_recv()
        out_v[a] = (part_own[a] + part_in[a].astype(F32)).astype(BF16)
        store = pltpu.make_async_copy(
            out_v.at[a], out_hbm.at[pl.ds(a * LANE, LANE)], store_sem.at[a]
        )
        store.start()
        stores.append(store)

    for store in stores:
        store.wait()
    for i in range(len(moves)):
        a2a_all(i).wait_send()
    for i in range(2):
        spread_all(i).wait_send()
        to_sibling(i).wait_send()
    for copy in near_copies + [swap_f, swap_s] + backs + swaps + parts:
        copy.wait_send()


def per_device(query_proj, key_proj, value_proj, filter_taps, skip_gain, out_weight):
    chips = lax.axis_size("ctx") // 2
    rows, width = query_proj.shape
    runs = rows // LANE
    side = width // 2
    half = chips * runs * 2
    tables = [jnp.asarray(t) for t in dft_tables(chips, runs)]
    gain = skip_gain[None, :]
    dma = pltpu.SemaphoreType.DMA

    def like(x):
        return pltpu.VMEM(x.shape, x.dtype)

    tall = runs * 2 * PART
    flat = pltpu.VMEM((SETS, chips, tall, LANE), BF16)
    swapped = pltpu.VMEM((runs, side, LANE), BF16)
    wide = pltpu.VMEM((chips * tall, LANE), F32)
    weights = pltpu.VMEM((2, width, width), BF16)
    piece = pltpu.VMEM((runs, LANE, width), BF16)
    moves = 1 + SETS + 1 + runs
    return pl.pallas_call(
        functools.partial(whole_kernel, chips, runs, width),
        out_shape=jax.ShapeDtypeStruct((rows, width), BF16),
        in_specs=[pl.BlockSpec(memory_space=pl.ANY)] * (6 + len(tables)),
        out_specs=pl.BlockSpec(memory_space=pl.ANY),
        scratch_shapes=[
            like(query_proj), like(key_proj), like(value_proj), like(filter_taps), like(gain),
            weights, weights,
            *[like(t) for t in tables],
            *[swapped] * 8,
            *[flat] * 6,
            wide, wide, pltpu.VMEM((SETS * PART, half, 2 * LANE), F32),
            piece, piece, piece, piece, pltpu.VMEM((runs, LANE, width), F32), piece,
            dma((7,)), dma((len(tables),)), dma((moves,)), dma((runs,)),
            dma((moves,)), dma((moves,)), dma((2 + runs,)), dma((2 + runs,)),
            dma((2,)), dma((2,)), dma((2,)), dma((2,)), dma((2,)), dma((2,)),
            dma((runs,)), dma((runs,)), dma((runs,)), dma((runs,)),
        ],
        compiler_params=pltpu.CompilerParams(
            collective_id=0, has_side_effects=True, vmem_limit_bytes=56 * 1024 * 1024
        ),
    )(query_proj, key_proj, value_proj, filter_taps, gain, out_weight, *tables)


def solution(mesh):
    placed = (
        P("ctx", "chan"),
        P("ctx", "chan"),
        P("ctx", "chan"),
        P("ctx", "chan"),
        P("chan"),
        P("chan", None),
    )
    return jax.shard_map(
        per_device, mesh=mesh, in_specs=placed, out_specs=P("ctx", "chan"), check_vma=False
    )
```

time: 135 us -> 123 us (0.911)
  the two profiles are of different devices: /device:TPU:102 before, /device:TPU:1 now
where the time goes in v3:
time: 123 us
  Pallas kernels  121 us (98%)
  local copies, waits for them, and re-layouts  2.06 us (2%)
    pallas_call x1, Pallas kernels, per_device(): pl.pallas_call(functools.partial(whole_kernel, chips, runs, width), out_s...  121 us

profile of v3, /device:TPU:1, one launch (start us, length us, event | category | flops | bytes accessed | tf_op | source)
XLA Modules:
  0.0 122.7 jit_solution(3168067809747104728)
XLA Ops:
  0.0 120.6 %shard_map.154 = bf16[384,1024]{1,0:T(8,128)(2,1)} custom-call(bf16[384,1024]{1,0:T(8,128)(2,1)} %q_hbm.1, bf16[384,1024]{1,0:T(8,128)(2,1)} %k_hbm.1, bf16[384,1024]{1,0:T(8,128)(2,1)} %v_hbm.1, f32[384,1024]{1,0:T(8,128)} %f_hbm.1, f32[1,1024]{1,0:T(1,128)} %bitcast.1, bf16[1024,4096]{1,0:T(8,128)(2,1)} %w_hbm.1, ...), custom_call_target="tpu_custom_call" | custom-call | tf_op jit(solution)/shard_map/pallas_call | solution.py:443
  120.6 2.1 %copy.18 = bf16[384,1024]{1,0:T(8,128)(2,1)} copy(bf16[384,1024]{1,0:T(8,128)(2,1)} %shard_map.154) | data formatting | bytes 1572864

commit v4 on v3

--- a/solution.py
+++ b/solution.py
@@ -59,13 +59,16 @@
 
 def dot3(x, m_hi, m_lo):
     hi, lo = split(x)
-    return dot(hi, m_hi) + dot(lo, m_hi) + dot(hi, m_lo)
+    count = x.shape[0]
+    both = dot(jnp.concatenate([hi, lo], 0), m_hi)
+    return both[:count] + both[count:] + dot(hi, m_lo)
 
 
 MESH = pl.DeviceIdType.MESH
 COLS = 256
 SETS = 2
 PART = 8
+PIECES = 2
 
 
 def whole_kernel(
@@ -285,8 +288,9 @@
             re = y[:half, j * LANE:(j + 1) * LANE]
             im = y[half:, j * LANE:(j + 1) * LANE]
             turned = jnp.concatenate([re * cos + im * sin, im * cos - re * sin], 1)
-            found.append(dot3(turned, fw_hi[...], fw_lo[...]))
-        return found
+            found.append(turned)
+        spec = dot3(jnp.concatenate(found, 0), fw_hi[...], fw_lo[...])
+        return [spec[j * half:(j + 1) * half] for j in range(len(chans))]
 
     def widen(src):
         wide_a[...] = src.astype(F32).reshape(chips * tall, LANE)
@@ -311,11 +315,16 @@
             chans = (2 * p, 2 * p + 1)
             cos, sin = cos_ref[...], sin_ref[...]
             backs = []
+            products = []
             for ch, s in zip(chans, spectra(wide_a, chans)):
                 f = spec_f[g * PART + ch]
                 s_re, s_im, f_re, f_im = s[:, :LANE], s[:, LANE:], f[:, :LANE], f[:, LANE:]
-                product = jnp.concatenate([s_re * f_re - s_im * f_im, s_re * f_im + s_im * f_re], 1)
-                z = dot3(product, iv_hi[...], iv_lo[...])
+                products.append(
+                    jnp.concatenate([s_re * f_re - s_im * f_im, s_re * f_im + s_im * f_re], 1)
+                )
+            back = dot3(jnp.concatenate(products, 0), iv_hi[...], iv_lo[...])
+            for j in range(len(chans)):
+                z = back[j * half:(j + 1) * half]
                 re, im = z[:, :LANE], z[:, LANE:]
                 backs.append(jnp.concatenate([re * cos - im * sin, im * cos + re * sin], 0))
             z_hi, z_lo = split(jnp.concatenate(backs, 1))
@@ -352,7 +361,10 @@
     a2a_arrived(3)
     swaps = []
     backs = []
-    for a in range(runs):
+    parts = []
+    step = LANE // PIECES
+
+    def gate_run(a):
         a2a_arrived(4 + a)
         tile = [recv_c[g, :, a * 2 * PART:(a + 1) * 2 * PART, :].astype(F32) for g in range(SETS)]
         other = jnp.concatenate([t[:, PART:] for t in tile], 1).reshape(side, LANE)
@@ -364,50 +376,72 @@
         gated(a, own, mine)
         back.wait_recv()
         gated(a, take_c[a].astype(F32), theirs)
-        swap = remote(g_own.at[a], g_near.at[a], g_send.at[a], g_recv.at[a], (c, near))
-        swap.start()
-        swaps.append(swap)
-
-    spread(0)
-
-    def product(i, a, piece):
+        for b in range(PIECES):
+            i = a * PIECES + b
+            here = pl.ds(b * step, step)
+            swap = remote(
+                g_own.at[a, here], g_near.at[a, here], g_send.at[i], g_recv.at[i], (c, near)
+            )
+            swap.start()
+            swaps.append(swap)
+
+    def product(i, a, here, piece):
         cols = pl.ds(pl.multiple_of(piece * COLS, COLS), COLS)
-        return cols, dot(g_own[a], w_own[i, :, cols]) + dot(g_near[a], w_near[i, :, cols])
-
-    to_sibling(1).wait_recv()
-    parts = []
+        return cols, dot(g_own[a, here], w_own[i, :, cols]) + dot(g_near[a, here], w_near[i, :, cols])
+
+    def project_run(a):
+        for b in range(PIECES):
+            i = a * PIECES + b
+            here = slice(b * step, (b + 1) * step)
+            swaps[i].wait_recv()
+
+            def project(piece, _):
+                cols, sums = product(1, a, here, piece)
+                part_out[a, here, cols] = sums.astype(BF16)
+                return 0
+
+            lax.fori_loop(0, width // COLS, project, 0)
+            rows = pl.ds(b * step, step)
+            part = remote(
+                part_out.at[a, rows], part_in.at[a, rows], p_send.at[i], p_recv.at[i], (c, far)
+            )
+            part.start()
+            parts.append(part)
+
     for a in range(runs):
-        swaps[a].wait_recv()
-
-        def project(piece, _, a=a):
-            cols, sums = product(1, a, piece)
-            part_out[a, :, cols] = sums.astype(BF16)
-            return 0
-
-        lax.fori_loop(0, width // COLS, project, 0)
-        part = remote(part_out.at[a], part_in.at[a], p_send.at[a], p_recv.at[a], (c, far))
-        part.start()
-        parts.append(part)
+        gate_run(a)
+        if a == runs - 1:
+            spread(0)
+        if a == 0:
+            to_sibling(1).wait_recv()
+        else:
+            project_run(a - 1)
+    project_run(runs - 1)
     spread_all(0).wait_recv()
     to_sibling(0).start()
     to_sibling(0).wait_recv()
     for a in range(runs):
 
         def project_own(piece, _, a=a):
-            cols, sums = product(0, a, piece)
+            cols, sums = product(0, a, slice(None), piece)
             part_own[a, :, cols] = sums
             return 0
 
         lax.fori_loop(0, width // COLS, project_own, 0)
     stores = []
     for a in range(runs):
-        parts[a].wait_recv()
-        out_v[a] = (part_own[a] + part_in[a].astype(F32)).astype(BF16)
-        store = pltpu.make_async_copy(
-            out_v.at[a], out_hbm.at[pl.ds(a * LANE, LANE)], store_sem.at[a]
-        )
-        store.start()
-        stores.append(store)
+        for b in range(PIECES):
+            i = a * PIECES + b
+            here = slice(b * step, (b + 1) * step)
+            parts[i].wait_recv()
+            out_v[a, here] = (part_own[a, here] + part_in[a, here].astype(F32)).astype(BF16)
+            store = pltpu.make_async_copy(
+                out_v.at[a, pl.ds(b * step, step)],
+                out_hbm.at[pl.ds(a * LANE + b * step, step)],
+                store_sem.at[i],
+            )
+            store.start()
+            stores.append(store)
 
     for store in stores:
         store.wait()
@@ -453,10 +487,10 @@
             *[flat] * 6,
             wide, wide, pltpu.VMEM((SETS * PART, half, 2 * LANE), F32),
             piece, piece, piece, piece, pltpu.VMEM((runs, LANE, width), F32), piece,
-            dma((7,)), dma((len(tables),)), dma((moves,)), dma((runs,)),
+            dma((7,)), dma((len(tables),)), dma((moves,)), dma((runs * PIECES,)),
             dma((moves,)), dma((moves,)), dma((2 + runs,)), dma((2 + runs,)),
             dma((2,)), dma((2,)), dma((2,)), dma((2,)), dma((2,)), dma((2,)),
-            dma((runs,)), dma((runs,)), dma((runs,)), dma((runs,)),
+            *[dma((runs * PIECES,))] * 4,
         ],
         compiler_params=pltpu.CompilerParams(
             collective_id=0, has_side_effects=True, vmem_limit_bytes=56 * 1024 * 1024

time: 123 us -> 120 us (0.976)
  Pallas kernels: 121 us -> 117 us
    pallas_call x1, Pallas kernels: 121 us -> 117 us  [per_device(): pl.pallas_call(functools.partial(whole_kernel, chips, runs, width), out_s...]
where the time goes in v4:
time: 120 us; the launch traced here: 119 us
  Pallas kernels  117 us (98%)
  local copies, waits for them, and re-layouts  2.06 us (2%)
    pallas_call x1, Pallas kernels, per_device(): pl.pallas_call(functools.partial(whole_kernel, chips, runs, width), out_s...  117 us

profile of v4, /device:TPU:1, one launch (start us, length us, event | category | flops | bytes accessed | tf_op | source)
XLA Modules:
  0.0 119.5 jit_solution(7273475436258710209)
XLA Ops:
  0.0 117.4 %shard_map.154 = bf16[384,1024]{1,0:T(8,128)(2,1)} custom-call(bf16[384,1024]{1,0:T(8,128)(2,1)} %q_hbm.1, bf16[384,1024]{1,0:T(8,128)(2,1)} %k_hbm.1, bf16[384,1024]{1,0:T(8,128)(2,1)} %v_hbm.1, f32[384,1024]{1,0:T(8,128)} %f_hbm.1, f32[1,1024]{1,0:T(1,128)} %bitcast.1, bf16[1024,4096]{1,0:T(8,128)(2,1)} %w_hbm.1, ...), custom_call_target="tpu_custom_call" | custom-call | tf_op jit(solution)/shard_map/pallas_call | solution.py:477
  117.4 2.1 %copy.18 = bf16[384,1024]{1,0:T(8,128)(2,1)} copy(bf16[384,1024]{1,0:T(8,128)(2,1)} %shard_map.154) | data formatting | bytes 1572864

commit v5 on v4

--- a/solution.py
+++ b/solution.py
@@ -68,7 +68,7 @@
 COLS = 256
 SETS = 2
 PART = 8
-PIECES = 2
+PIECES = 4
 
 
 def whole_kernel(
@@ -177,7 +177,11 @@
             return 0
 
         a2a_own(i).start()
-        lax.fori_loop(1, chips, send, 0)
+        if i < 3:
+            lax.fori_loop(1, chips, send, 0)
+        else:
+            lax.fori_loop(0, chips // 2, lambda j, _: send(2 * j + 1, 0), 0)
+            lax.fori_loop(1, chips // 2, lambda j, _: send(2 * j, 0), 0)
 
     def a2a_all(i):
         src, dst = moves[i][:2]

time: 120 us -> 119 us (level)
  no operation moved by 1% of the time
where the time goes in v5:
time: 119 us
  Pallas kernels  117 us (98%)
  local copies, waits for them, and re-layouts  2.06 us (2%)
    pallas_call x1, Pallas kernels, per_device(): pl.pallas_call(functools.partial(whole_kernel, chips, runs, width), out_s...  117 us

profile of v5, /device:TPU:1, one launch (start us, length us, event | category | flops | bytes accessed | tf_op | source)
XLA Modules:
  0.0 118.9 jit_solution(13752076093126677670)
XLA Ops:
  0.0 116.8 %shard_map.154 = bf16[384,1024]{1,0:T(8,128)(2,1)} custom-call(bf16[384,1024]{1,0:T(8,128)(2,1)} %q_hbm.1, bf16[384,1024]{1,0:T(8,128)(2,1)} %k_hbm.1, bf16[384,1024]{1,0:T(8,128)(2,1)} %v_hbm.1, f32[384,1024]{1,0:T(8,128)} %f_hbm.1, f32[1,1024]{1,0:T(1,128)} %bitcast.1, bf16[1024,4096]{1,0:T(8,128)(2,1)} %w_hbm.1, ...), custom_call_target="tpu_custom_call" | custom-call | tf_op jit(solution)/shard_map/pallas_call | solution.py:481
  116.8 2.1 %copy.18 = bf16[384,1024]{1,0:T(8,128)(2,1)} copy(bf16[384,1024]{1,0:T(8,128)(2,1)} %shard_map.154) | data formatting | bytes 1572864
